TPU v7x, 32 devices: a whole 2x2x4 slice. The times are simulated.
32 devices in a mesh: dp: 4 (over x, core), expert: 8 (over z, y).
Axes of the slice: x: 2, y: 2, z: 4, core: 2. Of those that a mesh axis runs over, the one named last changes fastest.
Arguments:
- cells: bfloat16 [8192, 1024], P(('dp', 'expert')), may hold values from -6 to 6
- cell_bins: int32 [8192], P(('dp', 'expert')), may hold values from 0 to 127
- tile_counts: int32 [32, 4], P(('dp', 'expert')), may hold values from 1 to 192, 256 in all within a row
- bin_base: bfloat16 [4096, 1024], P(('dp', 'expert')), may hold values from -6 to 6
- norm_gain: float32 [1024], replicated, may hold values from 0.1 to 1.9
- expert_ids: int32 [4096, 1], P(('dp', 'expert')), may hold values from 0 to 7; in each aligned block of 128 rows (0 to 127, 128 to 255, ...) at most 24 rows name the same one
- gate_q: bfloat16 [8, 4096, 1024], P('expert', 'dp'), may hold values from -0.1875 to 0.1875
- up_q: bfloat16 [8, 4096, 1024], P('expert', 'dp'), may hold values from -0.1875 to 0.1875
- down_q: bfloat16 [8, 4096, 1024], P('expert', 'dp'), may hold values from -0.09375 to 0.09375
- gate_scales: int32 [8, 32, 8], P('expert', 'dp'), may hold values from -1 to 1
- up_scales: int32 [8, 32, 8], P('expert', 'dp'), may hold values from -1 to 1
- down_scales: int32 [8, 32, 8], P('expert', 'dp'), may hold values from -1 to 1
Outputs:
- encoded: bfloat16 [4096, 1024], P(('dp', 'expert'))
Inputs may be any that keep to these rules, and one draw needn't show every extreme that they name: Each device's cells are stored grouped by tile in order of t; row s of tile_counts gives the lengths of these groups, sums to 256, and its largest entry is 192. `expert_ids`: among the 128 bins of one tile no expert is named more than 24 times, a bound that some block reaches.
All inputs are finite; a program needn't handle non-finite values.
Results may differ from a plain program's by a relative error of at most 0.014.
Values may be sent and summed in bfloat16 or wider, within the bound.
A program may use at most 64 MiB of HBM per device.

v0:
```python
import jax
import jax.numpy as jnp
from jax import lax
from jax.sharding import PartitionSpec as P

QB = 128


def dequantize(quant, scale):
    factor = jnp.exp2(scale.astype(jnp.float32))
    factor = jnp.repeat(jnp.repeat(factor, QB, axis=0), QB, axis=1).astype(jnp.bfloat16)
    return quant * factor


def on_device(
    cells,
    cell_bins,
    tile_counts,
    bin_base,
    norm_gain,
    expert_ids,
    gate_q,
    up_q,
    down_q,
    gate_scales,
    up_scales,
    down_scales,
):
    dp_size = lax.axis_size("dp")
    expert_count = lax.axis_size("expert") * gate_q.shape[0]
    cell_total = cells.shape[0]
    tile_bins = bin_base.shape[0]
    counts = tile_counts[0]
    run_ends = jnp.cumsum(counts)
    run_starts = run_ends - counts
    bin_iota = jnp.arange(tile_bins, dtype=jnp.int32)
    cell_cap = min(3 * cell_total // dp_size, cell_total - dp_size + 1)
    slot_iota = jnp.arange(cell_cap, dtype=jnp.int32)
    take_rows = jnp.clip(run_starts[:, None] + slot_iota[None, :], 0, cell_total - 1).reshape(-1)
    valid = (slot_iota[None, :] < counts[:, None]).reshape(-1)
    slot_rows = jnp.where(
        valid[:, None], jnp.take(cells, take_rows, axis=0), jnp.zeros((), jnp.bfloat16)
    )
    slot_bins = jnp.where(valid, jnp.take(cell_bins, take_rows), -1)
    got_rows, got_bins = (
        lax.all_to_all(slot_rows, "dp", split_axis=0, concat_axis=0, tiled=True),
        lax.all_to_all(slot_bins, "dp", split_axis=0, concat_axis=0, tiled=True),
    )
    matcher = (bin_iota[:, None] == got_bins[None, :]).astype(jnp.bfloat16)
    splat_sum = jnp.dot(matcher, got_rows, preferred_element_type=jnp.float32)
    residual_in = bin_base.astype(jnp.float32) + splat_sum
    mean_sq = jnp.mean(residual_in * residual_in, axis=1, keepdims=True)
    normed = (residual_in * lax.rsqrt(mean_sq + 1e-06) * norm_gain[None, :]).astype(jnp.bfloat16)
    capacity = max(2, 3 * tile_bins // (2 * expert_count))
    expert_col = expert_ids[:, 0]
    one_hot = (expert_col[:, None] == jnp.arange(expert_count, dtype=jnp.int32)[None, :]).astype(
        jnp.int32
    )
    within = jnp.sum(jnp.cumsum(one_hot, axis=0) * one_hot, axis=1) - 1
    slot_of = expert_col * capacity + within
    placer = (
        jnp.arange(expert_count * capacity, dtype=jnp.int32)[:, None] == slot_of[None, :]
    ).astype(jnp.bfloat16)
    outgoing = jnp.dot(placer, normed, preferred_element_type=jnp.float32).astype(jnp.bfloat16)
    arrived = lax.all_to_all(outgoing, "expert", split_axis=0, concat_axis=0, tiled=True)
    w_gate = dequantize(gate_q[0], gate_scales[0])
    w_up = dequantize(up_q[0], up_scales[0])
    w_down = dequantize(down_q[0], down_scales[0])
    contract = (((1,), (1,)), ((), ()))
    block_rows = lax.all_gather(arrived, "dp", axis=0, tiled=True)
    gate_val = lax.dot_general(block_rows, w_gate, contract, preferred_element_type=jnp.float32)
    up_val = lax.dot_general(block_rows, w_up, contract, preferred_element_type=jnp.float32)
    hidden = (jax.nn.silu(gate_val) * up_val).astype(jnp.bfloat16)
    partial_rows = jnp.dot(hidden, w_down, preferred_element_type=jnp.float32)
    summed = lax.psum_scatter(
        partial_rows.astype(jnp.bfloat16), "dp", scatter_dimension=0, tiled=True
    )
    returned = lax.all_to_all(summed, "expert", split_axis=0, concat_axis=0, tiled=True)
    expert_out = lax.dot_general(
        placer, returned, (((0,), (0,)), ((), ())), preferred_element_type=jnp.float32
    )
    return (residual_in + expert_out).astype(jnp.bfloat16)


def solution(mesh):
    placed = (
        P(("dp", "expert"), None),
        P(("dp", "expert")),
        P(("dp", "expert"), None),
        P(("dp", "expert"), None),
        P(),
        P(("dp", "expert"), None),
        P("expert", "dp", None),
        P("expert", "dp", None),
        P("expert", "dp", None),
        P("expert", "dp", None),
        P("expert", "dp", None),
        P("expert", "dp", None),
    )
    return jax.shard_map(
        on_device, mesh=mesh, in_specs=placed, out_specs=P(("dp", "expert"), None), check_vma=False
    )
```

profile of v0, /device:TPU:0, one launch (start us, length us, event | category | flops | bytes accessed | tf_op | source)
XLA Modules:
  0.0 157.9 jit_solution(16926775284610306466)
XLA Ops:
  6.5 0.0 copy-start
  6.5 0.0 copy-start.1
  6.5 0.9 reduce-window.8
  7.4 0.7 bitcast_subtract_fusion
  8.1 0.1 add_clamp_fusion
  8.2 0.1 min.18
  8.3 0.0 copy-done.1
  8.3 0.0 copy-start.8
  8.3 5.0 %gather_fusion = s32[768]{0:T(1024)S(1)} fusion(s32[256]{0:T(256)S(1)} %copy-done.1, s32[1024]{0:T(1024)S(1)} %pad_clamp_fusion), kind=kCustom, calls=%fused_computation | custom fusion | bytes 9216 | tf_op jit(solution)/shard_map/jit(_take)/gather | solution.py:44
  13.3 0.1 gather.13
  13.4 0.0 copy-done.8
  13.4 0.1 select_select_fusion.1
  13.5 0.6 copy.13
  14.1 4.2 %all-to-all-start = ((s32[4,192,1]{1,2,0:T(1,128)}), s32[4,192,1]{1,2,0:T(1,128)S(1)}, u32[]{:S(2)}, u32[]{:S(2)}) async-start(s32[4,192,1]{1,2,0:T(1,128)} %copy.13), calls=%async_computation | async-start | bytes 8192 | tf_op jit(solution)/shard_map/all_to_all | solution.py:47
  18.3 0.1 iota_compare_fusion.6
  18.4 0.0 copy-done
  18.4 2.8 %gather_fusion.1 = bf16[768,1024]{1,0:T(8,128)(2,1)S(1)} fusion(bf16[256,1024]{1,0:T(8,128)(2,1)S(1)} %copy-done, s32[1024]{0:T(1024)S(1)} %pad_clamp_fusion), kind=kCustom, calls=%fused_computation.1 | custom fusion | bytes 3148800 | tf_op jit(solution)/shard_map/jit(_take)/gather | solution.py:42
  21.2 1.5 select_select_fusion
  22.6 0.0 copy-start.7
  22.6 0.0 copy-start.2
  22.6 0.0 all-to-all-done
  22.7 3.7 %all-to-all-start.1 = ((bf16[4,192,1024]{2,1,0:T(8,128)(2,1)}), bf16[4,192,1024]{2,1,0:T(8,128)(2,1)S(1)}, u32[]{:S(2)}, u32[]{:S(2)}) async-start(bf16[4,192,1024]{2,1,0:T(8,128)(2,1)} %select_select_fusion), calls=%async_computation.1 | async-start | bytes 3145728 | tf_op jit(solution)/shard_map/all_to_all | solution.py:46
  26.4 0.0 copy-start.3
  26.4 0.0 all-gather.2.cloned.1.call-start
  26.4 0.0 copy-done.7
  26.4 0.1 fusion.14
  26.5 0.2 reduce_window_sum.18
  26.7 0.2 select_reduce_fusion
  26.9 0.1 eq.42
  27.0 19.4 %all-to-all-done.1 = bf16[4,192,1024]{2,1,0:T(8,128)(2,1)S(1)} async-done(((bf16[4,192,1024]{2,1,0:T(8,128)(2,1)}), bf16[4,192,1024]{2,1,0:T(8,128)(2,1)S(1)}, u32[]{:S(2)}, u32[]{:S(2)}) %all-to-all-start.1) | async-done | bytes 1572896 | tf_op jit(solution)/shard_map/all_to_all | solution.py:46
  46.4 0.0 copy-done.2
  46.4 0.0 copy-start.4
  46.4 0.0 copy-start.5
  46.4 0.0 copy-start.6
  46.4 0.5 multiply_reduce_fusion
  46.9 0.0 copy-done.3
  46.9 0.3 convolution_convert_fusion
  47.2 0.0 copy-start.9
  47.3 18.3 %all_to_all.39 = bf16[8,24,1024]{2,1,0:T(8,128)(2,1)} all-to-all(bf16[8,24,1024]{2,1,0:T(8,128)(2,1)S(1)} %bitcast.71), channel_id=1, replica_groups=mesh['dp'=4,'expert'=8] {'expert'}, dimensions={0} | all-to-all | bytes 786432 | tf_op jit(solution)/shard_map/all_to_all | solution.py:65
  65.5 0.0 all-gather.2.cloned.1.call-update
  65.5 0.0 reduce-scatter.2.cloned.1.call-start
  65.6 0.0 copy-done.4
  65.6 0.0 copy-done.5
  65.6 0.0 copy-done.6
  65.7 17.5 %all-gather.2.cloned.1.call-done = bf16[768,1024]{1,0:T(8,128)(2,1)} async-done(((bf16[192,1024]{1,0:T(8,128)(2,1)}), bf16[768,1024]{1,0:T(8,128)(2,1)}) %all-gather.2.cloned.1.call-update) | async-done | bytes 1572880 | tf_op jit(solution)/shard_map/all_gather | solution.py:70
  83.1 0.0 copy-start.10
  83.2 2.9 %broadcast_in_dim.69 = bf16[1024,8,128]{2,1,0:T(8,128)(2,1)S(1)} broadcast(bf16[1024,8]{1,0:T(8,128)(2,1)S(1)} %bitcast.73), dimensions={0,1} | broadcast | bytes 2113536 | tf_op jit(solution)/shard_map/broadcast_in_dim | solution.py:11
  86.1 0.0 copy-done.9
  86.1 0.0 copy-done.10
  86.1 3.5 %fusion.2 = f32[768,1024]{1,0:T(8,128)} fusion(bf16[768,1024]{1,0:T(8,128)(2,1)S(1)} %copy-done.10, bf16[128,8,8,128]{3,2,1,0:T(8,128)(2,1)S(1)} %bitcast.69, bf16[1,1024,1024]{2,1,0:T(8,128)(2,1)S(1)} %copy-done.9), kind=kOutput, calls=%fused_computation.7 | convolution fusion | flops 1611661312 | bytes 8912896 | tf_op jit(solution)/shard_map/dot_general | solution.py:72
  89.7 2.9 %broadcast_in_dim.67 = bf16[1024,8,128]{2,1,0:T(8,128)(2,1)S(1)} broadcast(bf16[1024,8]{1,0:T(8,128)(2,1)S(1)} %bitcast.74), dimensions={0,1} | broadcast | bytes 2113536 | tf_op jit(solution)/shard_map/broadcast_in_dim | solution.py:11
  92.7 2.2 %broadcast_in_dim.71 = bf16[1024,8,128]{2,1,0:T(8,128)(2,1)} broadcast(bf16[1024,8]{1,0:T(8,128)(2,1)S(1)} %bitcast.75), dimensions={0,1} | broadcast | bytes 2113536 | tf_op jit(solution)/shard_map/broadcast_in_dim | solution.py:11
  94.9 9.2 %fusion.9 = bf16[768,1024]{1,0:T(8,128)(2,1)} fusion(bf16[128,8,8,128]{3,2,1,0:T(8,128)(2,1)} %bitcast.68, bf16[1,1024,1024]{2,1,0:T(8,128)(2,1)} %param.20, f32[768,1024]{1,0:T(8,128)} %fusion.2, bf16[768,1024]{1,0:T(8,128)(2,1)} %all-gather.2.cloned.1.call-done, bf16[128,8,8,128]{3,2,1,0:T(8,128)(2,1)S(1)} %bitcast.67, bf16[1,1024,1024]{2,1,0:T(8,128)(2,1)} %param.18), kind=kOutput, calls=%fused_computation.15 | convolution fusion | flops 3228827648 | bytes 14680064 | tf_op jit(solution)/shard_map/dot_general | solution.py:74
  104.1 0.0 reduce-scatter.2.cloned.1.call-update
  104.1 28.3 %reduce-scatter.2.cloned.1.call-done = bf16[192,1024]{1,0:T(8,128)(2,1)} async-done(((bf16[768,1024]{1,0:T(8,128)(2,1)}), bf16[192,1024]{1,0:T(8,128)(2,1)}) %reduce-scatter.2.cloned.1.call-update) | async-done | bytes 393232 | tf_op jit(solution)/shard_map/reduce_scatter | solution.py:75
  132.4 17.6 %all_to_all.40 = bf16[8,24,1024]{2,1,0:T(8,128)(2,1)S(1)} all-to-all(bf16[8,24,1024]{2,1,0:T(8,128)(2,1)} %bitcast.76), channel_id=1, replica_groups=mesh['dp'=4,'expert'=8] {'expert'}, dimensions={0} | all-to-all | bytes 786432 | tf_op jit(solution)/shard_map/all_to_all | solution.py:78
  150.1 1.0 fusion.10
  (11 shorter events, 0.2 us)
Async XLA Ops:
  6.5 11.8 %copy-start = (bf16[256,1024]{1,0:T(8,128)(2,1)S(1)}, bf16[256,1024]{1,0:T(8,128)(2,1)}, u32[]{:S(2)}) copy-start(bf16[256,1024]{1,0:T(8,128)(2,1)} %param.12) | copy-start | bytes 1572868
  6.5 1.8 %copy-start.1 = (s32[256]{0:T(256)S(1)}, s32[256]{0:T(256)}, u32[]{:S(2)}) copy-start(s32[256]{0:T(256)} %param.13) | copy-start | bytes 3076
  8.3 5.1 %copy-start.8 = (s32[1,4]{1,0:T(1,128)S(1)}, s32[1,4]{1,0:T(1,128)}, u32[]{:S(2)}) copy-start(s32[1,4]{1,0:T(1,128)} %param.14) | copy-start | bytes 52
  14.1 8.6 %all-to-all-start = ((s32[4,192,1]{1,2,0:T(1,128)}), s32[4,192,1]{1,2,0:T(1,128)S(1)}, u32[]{:S(2)}, u32[]{:S(2)}) async-start(s32[4,192,1]{1,2,0:T(1,128)} %copy.13), calls=%async_computation | async-start | bytes 8192 | tf_op jit(solution)/shard_map/all_to_all | solution.py:47
  22.6 3.8 %copy-start.7 = (s32[128,1]{0,1:T(1,128)S(1)}, s32[128,1]{0,1:T(1,128)}, u32[]{:S(2)}) copy-start(s32[128,1]{0,1:T(1,128)} %param.17) | copy-start | bytes 1540
  22.6 23.8 %copy-start.2 = (bf16[128,1024]{1,0:T(8,128)(2,1)S(1)}, bf16[128,1024]{1,0:T(8,128)(2,1)}, u32[]{:S(2)}) copy-start(bf16[128,1024]{1,0:T(8,128)(2,1)} %param.15) | copy-start | bytes 786436
  22.7 23.8 %all-to-all-start.1 = ((bf16[4,192,1024]{2,1,0:T(8,128)(2,1)}), bf16[4,192,1024]{2,1,0:T(8,128)(2,1)S(1)}, u32[]{:S(2)}, u32[]{:S(2)}) async-start(bf16[4,192,1024]{2,1,0:T(8,128)(2,1)} %select_select_fusion), calls=%async_computation.1 | async-start | bytes 3145728 | tf_op jit(solution)/shard_map/all_to_all | solution.py:46
  26.4 20.5 %copy-start.3 = (f32[1024]{0:T(1024)S(1)}, f32[1024]{0:T(1024)}, u32[]{:S(2)}) copy-start(f32[1024]{0:T(1024)} %param.16) | copy-start | bytes 12292
  26.4 56.8 %all-gather.2.cloned.1.call-start = ((), (), s32[]{:S(2)}) async-start(), calls=%async_computation.5 | async-start | bytes 1966080 | tf_op jit(solution)/shard_map/all_gather | solution.py:70
  46.4 19.2 %copy-start.4 = (s32[1,8,8]{2,1,0:T(8,128)S(1)}, s32[1,8,8]{2,1,0:T(8,128)}, u32[]{:S(2)}) copy-start(s32[1,8,8]{2,1,0:T(8,128)} %param.21) | copy-start | bytes 772
  46.4 19.2 %copy-start.5 = (s32[1,8,8]{2,1,0:T(8,128)S(1)}, s32[1,8,8]{2,1,0:T(8,128)}, u32[]{:S(2)}) copy-start(s32[1,8,8]{2,1,0:T(8,128)} %param.22) | copy-start | bytes 772
  46.4 19.2 %copy-start.6 = (s32[1,8,8]{2,1,0:T(8,128)S(1)}, s32[1,8,8]{2,1,0:T(8,128)}, u32[]{:S(2)}) copy-start(s32[1,8,8]{2,1,0:T(8,128)} %param.23) | copy-start | bytes 772
  47.2 38.9 %copy-start.9 = (bf16[1,1024,1024]{2,1,0:T(8,128)(2,1)S(1)}, bf16[1,1024,1024]{2,1,0:T(8,128)(2,1)}, u32[]{:S(2)}) copy-start(bf16[1,1024,1024]{2,1,0:T(8,128)(2,1)} %param.19) | copy-start | bytes 6291460
  65.5 66.9 %reduce-scatter.2.cloned.1.call-start = ((), (), s32[]{:S(2)}) async-start(), calls=%async_computation.6 | async-start | bytes 1966080 | tf_op jit(solution)/shard_map/reduce_scatter | solution.py:75
  83.1 3.0 %copy-start.10 = (bf16[768,1024]{1,0:T(8,128)(2,1)S(1)}, bf16[768,1024]{1,0:T(8,128)(2,1)}, u32[]{:S(2)}) copy-start(bf16[768,1024]{1,0:T(8,128)(2,1)} %all-gather.2.cloned.1.call-done) | copy-start | bytes 4718596
Sparse Core Ops, SparseCore 0:
  65.7 17.4 all-gather.1
  104.2 28.1 reduce-scatter.1
where the time goes:
time: 158 us
  waiting for transfers between devices  65.3 us (41%)
  blocking collectives  35.9 us (23%)
  local copies, waits for them, and re-layouts  16.9 us (11%)
  matrix products  14.5 us (9%)
  between operations  13.6 us (9%)
  starting transfers between devices  7.98 us (5%)
  other arithmetic  3.76 us (2%)
    reduce_scatter x1, waiting for transfers between devices, on_device(): lax.psum_scatter(partial_rows.astype(jnp.bfloat16), 'dp', scatter_dimensi...  28.3 us
    all_to_all x1, waiting for transfers between devices, on_device(): lax.all_to_all(slot_rows, 'dp', split_axis=0, concat_axis=0, tiled=True)  19.4 us
    all_to_all x1, blocking collectives, on_device(): lax.all_to_all(outgoing, 'expert', split_axis=0, concat_axis=0, tiled=True)  18.3 us
    all_to_all x1, blocking collectives, on_device(): lax.all_to_all(summed, 'expert', split_axis=0, concat_axis=0, tiled=True)  17.6 us
    all_gather x1, waiting for transfers between devices, on_device(): block_rows = lax.all_gather(arrived, 'dp', axis=0, tiled=True)  17.5 us
    dot_general x1, matrix products, on_device(): partial_rows = jnp.dot(hidden, w_down, preferred_element_type=jnp.float32)  9.2 us
    broadcast_in_dim x3, local copies, waits for them, and re-layouts, dequantize(): jnp.repeat(jnp.repeat(factor, QB, axis=0), QB, axis=1).astype(jnp.bfloat16)  8.11 us
    gather x2, local copies, waits for them, and re-layouts, on_device(): slot_bins = jnp.where(valid, jnp.take(cell_bins, take_rows), -1)  5.06 us
  transfers between devices with their start and end apart: 4, of which 3 were waited for; matrix products, arithmetic and copies ran while one was open for 3% of the time, Pallas kernels for 0%

commit v1 on v0

--- a/solution.py
+++ b/solution.py
@@ -1,6 +1,8 @@
 import jax
 import jax.numpy as jnp
 from jax import lax
+from jax.experimental import pallas as pl
+from jax.experimental.pallas import tpu as pltpu
 from jax.sharding import PartitionSpec as P
 
 QB = 128
@@ -82,7 +84,329 @@
     return (residual_in + expert_out).astype(jnp.bfloat16)
 
 
+MESH = pl.DeviceIdType.MESH
+BLK = 48
+NSEM = 41
+
+
+def flip(value, bits):
+    if bits == 1:
+        return (value + 1) % 2
+    high, low = value // 2, value % 2
+    return 2 * ((high + bits // 2) % 2) + (low + bits % 2) % 2
+
+
+def fused(
+    cells, bins, counts, base, gain, ids, wg_hbm, wu_hbm, wd_hbm, sg, su, sd,
+    out,
+    wg, wu, wd, ids_mine, ids_sib, part, part_sib, part_x_out, part_x, resid, both,
+    place, place_t, outgoing, rows_in, hidden, y32, y16, y_sib, q_out, q_in, final, back,
+    send, recv, wsem,
+):
+    dp, ex = lax.axis_index("dp"), lax.axis_index("expert")
+    x, c, z, y = dp // 2, dp % 2, ex // 2, ex % 2
+    sib = (2 * x + flip(c, 1), ex)
+    xpeer = (2 * flip(x, 1) + c, ex)
+    y_mine = (y + c) % 2
+    y_sibs = (y + 1 + c) % 2
+    zk = [z] + [2 * ((z // 2 + k // 2) % 2) + (z % 2 + k % 2) % 2 for k in (1, 2, 3)]
+    peer = [(dp, 2 * zk[k] + y_mine) for k in range(4)]
+
+    loads = [
+        pltpu.make_async_copy(src.at[0], dst, wsem.at[n])
+        for n, (src, dst) in enumerate(((wg_hbm, wg), (wu_hbm, wu), (wd_hbm, wd)))
+    ]
+    for load in loads:
+        load.start()
+
+    barrier = pltpu.get_barrier_semaphore()
+    for where in [sib, xpeer] + peer[1:]:
+        pl.semaphore_signal(barrier, inc=1, device_id=where, device_id_type=MESH)
+
+    @pl.when(c == 1)
+    def _():
+        pl.semaphore_signal(barrier, inc=1, device_id=peer[0], device_id_type=MESH)
+
+    def rdma(src, dst, n, where):
+        return pltpu.make_async_remote_copy(
+            src_ref=src, dst_ref=dst, send_sem=send.at[n], recv_sem=recv.at[n],
+            device_id=where, device_id_type=MESH,
+        )
+
+    f32, bf16 = jnp.float32, jnp.bfloat16
+    ids_mine[...] = jnp.broadcast_to(ids[...], (8, 128))
+
+    cell_iota = lax.broadcasted_iota(jnp.int32, (1, 256), 1)
+    tile = jnp.zeros((1, 256), jnp.int32)
+    run = jnp.zeros((1, 1), jnp.int32)
+    for t in range(4):
+        run = run + counts[:, t : t + 1]
+        tile = tile + (cell_iota >= run).astype(jnp.int32)
+    key = tile * 128 + bins[...]
+    row_iota = lax.broadcasted_iota(jnp.int32, (128, 256), 0)
+
+    def partial_of(t):
+        hit = (row_iota + 128 * t == key).astype(f32).astype(bf16)
+        return jnp.dot(hit, cells[...], preferred_element_type=f32)
+
+    other_x, other_c = flip(x, 1), flip(c, 1)
+    part[0] = partial_of(2 * other_x + other_c).astype(bf16)
+
+    pl.semaphore_wait(barrier, 5 + c)
+
+    c_p0 = rdma(part.at[0], part_sib.at[0], 1, sib)
+    c_p0.start()
+    c_ids = rdma(ids_mine, ids_sib, 0, sib)
+    c_ids.start()
+    part[1] = partial_of(2 * x + other_c).astype(bf16)
+    c_p1 = rdma(part.at[1], part_sib.at[1], 2, sib)
+    c_p1.start()
+    cross = partial_of(2 * other_x + c)
+    c_p0.wait_recv()
+    part_x_out[...] = (cross + part_sib[0].astype(f32)).astype(bf16)
+    c_px = rdma(part_x_out, part_x, 3, xpeer)
+    c_px.start()
+    resid[...] = base[...].astype(f32) + partial_of(2 * x + c)
+
+    spread = (
+        lax.broadcasted_iota(jnp.int32, (8, 1024), 1) // 128
+        == lax.broadcasted_iota(jnp.int32, (8, 1024), 0)
+    ).astype(f32)
+    for n, (w, s) in enumerate(((wg, sg), (wu, su), (wd, sd))):
+        loads[n].wait()
+        factor = jnp.dot(
+            jnp.exp2(s[0].astype(f32)).astype(bf16), spread.astype(bf16), preferred_element_type=f32
+        ).astype(bf16)
+        for b in range(8):
+            w[b * 128 : (b + 1) * 128, :] = w[b * 128 : (b + 1) * 128, :] * jnp.broadcast_to(
+                factor[b : b + 1, :], (128, 1024)
+            )
+
+    c_ids.wait_recv()
+    earlier = (
+        lax.broadcasted_iota(jnp.int32, (128, 128), 0)
+        < lax.broadcasted_iota(jnp.int32, (128, 128), 1)
+    ).astype(f32)
+
+    def slot_of(which):
+        named = (lax.broadcasted_iota(jnp.int32, (8, 128), 0) == which).astype(f32)
+        before = jnp.dot(
+            named.astype(bf16), earlier.astype(bf16), preferred_element_type=f32
+        )
+        return jnp.sum(named * before, axis=0, keepdims=True)
+
+    mine, theirs = ids_mine[...], ids_sib[...]
+    slot_mine = slot_of(mine) + (24 * c).astype(f32)
+    slot_theirs = slot_of(theirs) + (24 * other_c).astype(f32)
+    slot_iota = lax.broadcasted_iota(jnp.int32, (BLK, 128), 0).astype(f32)
+
+    def placer(which, slots, expert):
+        return jnp.where(
+            jnp.broadcast_to(which[0:1] == expert, (BLK, 128)),
+            (slot_iota == slots).astype(f32),
+            0.0,
+        )
+
+    for k in range(4):
+        here, there = 2 * zk[k] + y_mine, 2 * zk[k] + y_sibs
+        at = slice(k * BLK, (k + 1) * BLK)
+        own = placer(mine, slot_mine, here)
+        place[at, 0:128] = own.astype(bf16)
+        place[at, 128:256] = placer(theirs, slot_theirs, here).astype(bf16)
+        pair = jnp.concatenate([own, placer(mine, slot_mine, there)], axis=0)
+        place_t[k] = jnp.transpose(pair).astype(bf16)
+
+    c_p1.wait_recv()
+    resid[...] = resid[...] + part_sib[1].astype(f32)
+    c_px.wait_recv()
+    total = resid[...] + part_x[...].astype(f32)
+    resid[...] = total
+    mean_sq = jnp.mean(total * total, axis=1, keepdims=True)
+    both[0:128, :] = (total * lax.rsqrt(mean_sq + 1e-06) * gain[...]).astype(bf16)
+    c_n = rdma(both.at[0:128], both.at[128:256], 4, sib)
+    c_n.start()
+    c_n.wait_recv()
+    outgoing[...] = jnp.dot(place[...], both[...], preferred_element_type=f32).astype(bf16)
+
+    def slot(ref, k, s):
+        return ref.at[k, pl.ds(s * BLK, BLK)]
+
+    c_a = [rdma(outgoing.at[pl.ds(k * BLK, BLK)], slot(rows_in, k, 0), 5 + k, peer[k]) for k in range(4)]
+    f_s1 = [rdma(slot(rows_in, k, 0), slot(rows_in, k, 1), 9 + k, sib) for k in range(4)]
+    f_x2 = [rdma(slot(rows_in, k, 0), slot(rows_in, k, 2), 13 + k, xpeer) for k in range(4)]
+    f_s3 = [rdma(slot(rows_in, k, 2), slot(rows_in, k, 3), 17 + k, sib) for k in range(4)]
+    r_s2 = [rdma(slot(y16, k, 1), slot(y_sib, k, 1), 21 + k, sib) for k in range(4)]
+    r_s0 = [rdma(slot(y16, k, 0), slot(y_sib, k, 0), 25 + k, sib) for k in range(4)]
+    r_x0 = [rdma(q_out.at[k], q_in.at[k], 29 + k, xpeer) for k in range(4)]
+    b_a = [rdma(final.at[k], slot(back, k, 0), 33 + k, peer[k]) for k in range(4)]
+    b_s = [rdma(slot(back, k, 0), slot(back, k, 1), 37 + k, sib) for k in range(4)]
+
+    @pl.when(c == 1)
+    def _():
+        c_a[0].start()
+
+    for k in (1, 2, 3):
+        c_a[k].start()
+
+    @pl.when(c == 0)
+    def _():
+        rows_in[0, 0:BLK, :] = outgoing[0:BLK, :]
+
+    def arrive(k):
+        if k == 0:
+
+            @pl.when(c == 1)
+            def _():
+                c_a[0].wait_recv()
+
+        else:
+            c_a[k].wait_recv()
+        f_x2[k].start()
+        f_s1[k].start()
+
+    def ffn(k):
+        rows = rows_in[k]
+        contract = (((1,), (1,)), ((), ()))
+        for j in range(0, 1024, 256):
+            gate = lax.dot_general(rows, wg[j : j + 256, :], contract, preferred_element_type=f32)
+            up = lax.dot_general(rows, wu[j : j + 256, :], contract, preferred_element_type=f32)
+            hidden[:, j : j + 256] = (gate / (1.0 + jnp.exp(-gate)) * up).astype(bf16)
+        for j in range(0, 1024, 256):
+            res = jnp.dot(hidden[...], wd[:, j : j + 256], preferred_element_type=f32)
+            y16[k, 0:BLK, j : j + 256] = res[BLK : 2 * BLK].astype(bf16)
+            y16[k, BLK : 2 * BLK, j : j + 256] = res[3 * BLK :].astype(bf16)
+            y32[k, 0:BLK, j : j + 256] = res[0:BLK]
+            y32[k, BLK : 2 * BLK, j : j + 256] = res[2 * BLK : 3 * BLK]
+        r_s2[k].start()
+        r_s0[k].start()
+
+    def cross_sum(k):
+        r_s2[k].wait_recv()
+        q_out[k] = (y32[k, BLK : 2 * BLK, :] + y_sib[k, BLK : 2 * BLK, :].astype(f32)).astype(bf16)
+        r_x0[k].start()
+
+    def finish(k):
+        r_s0[k].wait_recv()
+        r_x0[k].wait_recv()
+        val = y32[k, 0:BLK, :] + y_sib[k, 0:BLK, :].astype(f32) + q_in[k].astype(f32)
+        final[k] = val.astype(bf16)
+        if k == 0:
+
+            @pl.when(c == 1)
+            def _():
+                b_a[0].start()
+
+            @pl.when(c == 0)
+            def _():
+                back[0, 0:BLK, :] = final[0]
+
+        else:
+            b_a[k].start()
+
+    def returned(k):
+        if k == 0:
+
+            @pl.when(c == 1)
+            def _():
+                b_a[0].wait_recv()
+
+        else:
+            b_a[k].wait_recv()
+        b_s[k].start()
+
+    arrive(0)
+    for k in range(4):
+        if k < 3:
+            arrive(k + 1)
+        f_x2[k].wait_recv()
+        f_s3[k].start()
+        f_s1[k].wait_recv()
+        f_s3[k].wait_recv()
+        ffn(k)
+        if k >= 1:
+            cross_sum(k - 1)
+        if k >= 2:
+            finish(k - 2)
+    cross_sum(3)
+    finish(2)
+    returned(0)
+    returned(1)
+    finish(3)
+    returned(2)
+    acc = resid[...]
+    for k in range(4):
+        if k == 3:
+            returned(3)
+        b_s[k].wait_recv()
+        acc = acc + jnp.dot(place_t[k], back[k], preferred_element_type=f32)
+    out[...] = acc.astype(bf16)
+
+    for copy in [c_ids, c_p0, c_p1, c_px, c_n] + f_s1 + f_x2 + f_s3 + r_s2 + r_s0 + r_x0 + b_s:
+        copy.wait_send()
+    for copy in c_a[1:] + b_a[1:]:
+        copy.wait_send()
+
+    @pl.when(c == 1)
+    def _():
+        c_a[0].wait_send()
+        b_a[0].wait_send()
+
+
+def on_device_fused(
+    cells, cell_bins, tile_counts, bin_base, norm_gain, expert_ids,
+    gate_q, up_q, down_q, gate_scales, up_scales, down_scales,
+):
+    bf16, f32 = jnp.bfloat16, jnp.float32
+    vmem, hbm = pl.BlockSpec(memory_space=pltpu.VMEM), pl.BlockSpec(memory_space=pl.ANY)
+    d = 1024
+    scratch = [
+        pltpu.VMEM((d, d), bf16),
+        pltpu.VMEM((d, d), bf16),
+        pltpu.VMEM((d, d), bf16),
+        pltpu.VMEM((8, 128), jnp.int32),
+        pltpu.VMEM((8, 128), jnp.int32),
+        pltpu.VMEM((2, 128, d), bf16),
+        pltpu.VMEM((2, 128, d), bf16),
+        pltpu.VMEM((128, d), bf16),
+        pltpu.VMEM((128, d), bf16),
+        pltpu.VMEM((128, d), f32),
+        pltpu.VMEM((256, d), bf16),
+        pltpu.VMEM((4 * BLK, 256), bf16),
+        pltpu.VMEM((4, 128, 2 * BLK), bf16),
+        pltpu.VMEM((4 * BLK, d), bf16),
+        pltpu.VMEM((4, 4 * BLK, d), bf16),
+        pltpu.VMEM((4 * BLK, d), bf16),
+        pltpu.VMEM((4, 2 * BLK, d), f32),
+        pltpu.VMEM((4, 2 * BLK, d), bf16),
+        pltpu.VMEM((4, 2 * BLK, d), bf16),
+        pltpu.VMEM((4, BLK, d), bf16),
+        pltpu.VMEM((4, BLK, d), bf16),
+        pltpu.VMEM((4, BLK, d), bf16),
+        pltpu.VMEM((4, 2 * BLK, d), bf16),
+        pltpu.SemaphoreType.DMA((NSEM,)),
+        pltpu.SemaphoreType.DMA((NSEM,)),
+        pltpu.SemaphoreType.DMA((3,)),
+    ]
+    return pl.pallas_call(
+        fused,
+        out_shape=jax.ShapeDtypeStruct(bin_base.shape, bf16),
+        in_specs=[vmem] * 6 + [hbm] * 3 + [vmem] * 3,
+        out_specs=vmem,
+        scratch_shapes=scratch,
+        compiler_params=pltpu.CompilerParams(
+            collective_id=0, has_side_effects=True, vmem_limit_bytes=48 * 1024 * 1024
+        ),
+        cost_estimate=pl.CostEstimate(
+            flops=6 * 768 * d * d, bytes_accessed=8 * d * d, transcendentals=768 * d
+        ),
+    )(
+        cells, cell_bins.reshape(1, -1), tile_counts, bin_base, norm_gain.reshape(1, -1),
+        expert_ids.reshape(1, -1), gate_q, up_q, down_q, gate_scales, up_scales, down_scales,
+    )
+
+
 def solution(mesh):
+    small = mesh.shape["dp"] == 4 and mesh.shape["expert"] == 8
     placed = (
         P(("dp", "expert"), None),
         P(("dp", "expert")),
@@ -98,5 +422,5 @@
         P("expert", "dp", None),
     )
     return jax.shard_map(
-        on_device, mesh=mesh, in_specs=placed, out_specs=P(("dp", "expert"), None), check_vma=False
-    )
+        on_device_fused if small else on_device, mesh=mesh, in_specs=placed, out_specs=P(("dp", "expert"), None), check_vma=False
+    )

time: 158 us -> 63.4 us (0.40)
  the two profiles are of different devices: /device:TPU:0 before, /device:TPU:3 now
where the time goes in v1:
time: 63.4 us; the launch traced here: 63 us
  Pallas kernels  52.4 us (83%)
  local copies, waits for them, and re-layouts  10.6 us (17%)
    pallas_call x1, Pallas kernels, on_device_fused(): pl.pallas_call(fused, out_shape=jax.ShapeDtypeStruct(bin_base.shape, bf16...  52.4 us
    unnamed x23, local copies, waits for them, and re-layouts  10.6 us

profile of v1, /device:TPU:3, one launch (start us, length us, event | category | flops | bytes accessed | tf_op | source)
XLA Modules:
  0.0 63.0 jit_solution(5135221065504059326)
XLA Ops:
  0.0 0.0 copy-start
  0.0 1.6 %copy-done = bf16[1,1024,1024]{2,1,0:T(8,128)(2,1)S(1)} copy-done((bf16[1,1024,1024]{2,1,0:T(8,128)(2,1)S(1)}, bf16[1,1024,1024]{2,1,0:T(8,128)(2,1)}, u32[]{:S(2)}) %copy-start) | copy-done | bytes 2097176
  1.6 0.0 copy-start.1
  1.6 1.6 %copy-done.1 = bf16[1,1024,1024]{2,1,0:T(8,128)(2,1)S(1)} copy-done((bf16[1,1024,1024]{2,1,0:T(8,128)(2,1)S(1)}, bf16[1,1024,1024]{2,1,0:T(8,128)(2,1)}, u32[]{:S(2)}) %copy-start.1) | copy-done | bytes 2097176
  3.2 0.0 copy-start.2
  3.2 1.0 %copy-done.2 = bf16[256,1024]{1,0:T(8,128)(2,1)S(1)} copy-done((bf16[256,1024]{1,0:T(8,128)(2,1)S(1)}, bf16[256,1024]{1,0:T(8,128)(2,1)}, u32[]{:S(2)}) %copy-start.2) | copy-done | bytes 524312
  4.2 0.0 copy-start.3
  4.2 0.9 %copy-done.3 = bf16[128,1024]{1,0:T(8,128)(2,1)S(1)} copy-done((bf16[128,1024]{1,0:T(8,128)(2,1)S(1)}, bf16[128,1024]{1,0:T(8,128)(2,1)}, u32[]{:S(2)}) %copy-start.3) | copy-done | bytes 262168
  5.2 0.0 copy-start.4
  5.2 0.7 %copy-done.4 = f32[1024]{0:T(1024)S(1)} copy-done((f32[1024]{0:T(1024)S(1)}, f32[1024]{0:T(1024)}, u32[]{:S(2)}) %copy-start.4) | copy-done | bytes 4120
  5.9 0.0 copy-start.5
  5.9 0.7 %copy-done.5 = s32[1,8,8]{2,1,0:T(8,128)S(1)} copy-done((s32[1,8,8]{2,1,0:T(8,128)S(1)}, s32[1,8,8]{2,1,0:T(8,128)}, u32[]{:S(2)}) %copy-start.5) | copy-done | bytes 280
  6.6 0.0 copy-start.6
  6.6 0.7 %copy-done.6 = s32[1,8,8]{2,1,0:T(8,128)S(1)} copy-done((s32[1,8,8]{2,1,0:T(8,128)S(1)}, s32[1,8,8]{2,1,0:T(8,128)}, u32[]{:S(2)}) %copy-start.6) | copy-done | bytes 280
  7.2 0.0 copy-start.7
  7.2 0.7 %copy-done.7 = s32[1,8,8]{2,1,0:T(8,128)S(1)} copy-done((s32[1,8,8]{2,1,0:T(8,128)S(1)}, s32[1,8,8]{2,1,0:T(8,128)}, u32[]{:S(2)}) %copy-start.7) | copy-done | bytes 280
  7.9 0.0 copy-start.8
  7.9 0.7 %copy-done.8 = s32[256]{0:T(256)S(1)} copy-done((s32[256]{0:T(256)S(1)}, s32[256]{0:T(256)}, u32[]{:S(2)}) %copy-start.8) | copy-done | bytes 1048
  8.6 0.0 copy-start.9
  8.6 0.7 %copy-done.9 = s32[1,4]{1,0:T(1,128)S(1)} copy-done((s32[1,4]{1,0:T(1,128)S(1)}, s32[1,4]{1,0:T(1,128)}, u32[]{:S(2)}) %copy-start.9) | copy-done | bytes 40
  9.3 0.0 copy-start.10
  9.3 0.7 %copy-done.10 = s32[128,1]{0,1:T(1,128)S(1)} copy-done((s32[128,1]{0,1:T(1,128)S(1)}, s32[128,1]{0,1:T(1,128)}, u32[]{:S(2)}) %copy-start.10) | copy-done | bytes 536
  9.9 52.4 %shard_map.118 = bf16[128,1024]{1,0:T(8,128)(2,1)S(1)} custom-call(bf16[256,1024]{1,0:T(8,128)(2,1)S(1)} %copy-done.2, s32[1,256]{1,0:T(1,128)S(1)} %bitcast.4, s32[1,4]{1,0:T(1,128)S(1)} %copy-done.9, bf16[128,1024]{1,0:T(8,128)(2,1)S(1)} %copy-done.3, f32[1,1024]{1,0:T(1,128)S(1)} %bitcast.3, s32[1,128]{1,0:T(1,128)S(1)} %bitcast.5, ...), custom_call_target="tpu_custom_call" | custom-call | flops 4831838208 | bytes 8388608 | tf_op jit(solution)/shard_map/pallas_call | solution.py:390
  62.3 0.7 %copy.14 = bf16[128,1024]{1,0:T(8,128)(2,1)} copy(bf16[128,1024]{1,0:T(8,128)(2,1)S(1)} %shard_map.118) | data formatting | bytes 524288
Async XLA Ops:
  0.0 1.6 %copy-start = (bf16[1,1024,1024]{2,1,0:T(8,128)(2,1)S(1)}, bf16[1,1024,1024]{2,1,0:T(8,128)(2,1)}, u32[]{:S(2)}) copy-start(bf16[1,1024,1024]{2,1,0:T(8,128)(2,1)} %wg_hbm.1) | copy-start | bytes 6291460
  1.6 1.6 %copy-start.1 = (bf16[1,1024,1024]{2,1,0:T(8,128)(2,1)S(1)}, bf16[1,1024,1024]{2,1,0:T(8,128)(2,1)}, u32[]{:S(2)}) copy-start(bf16[1,1024,1024]{2,1,0:T(8,128)(2,1)} %wu_hbm.1) | copy-start | bytes 6291460
  3.2 1.0 %copy-start.2 = (bf16[256,1024]{1,0:T(8,128)(2,1)S(1)}, bf16[256,1024]{1,0:T(8,128)(2,1)}, u32[]{:S(2)}) copy-start(bf16[256,1024]{1,0:T(8,128)(2,1)} %cells.1) | copy-start | bytes 1572868
  4.2 0.9 %copy-start.3 = (bf16[128,1024]{1,0:T(8,128)(2,1)S(1)}, bf16[128,1024]{1,0:T(8,128)(2,1)}, u32[]{:S(2)}) copy-start(bf16[128,1024]{1,0:T(8,128)(2,1)} %base.1) | copy-start | bytes 786436
  5.2 0.7 %copy-start.4 = (f32[1024]{0:T(1024)S(1)}, f32[1024]{0:T(1024)}, u32[]{:S(2)}) copy-start(f32[1024]{0:T(1024)} %param.16) | copy-start | bytes 12292
  5.9 0.7 %copy-start.5 = (s32[1,8,8]{2,1,0:T(8,128)S(1)}, s32[1,8,8]{2,1,0:T(8,128)}, u32[]{:S(2)}) copy-start(s32[1,8,8]{2,1,0:T(8,128)} %sg.1) | copy-start | bytes 772
  6.6 0.7 %copy-start.6 = (s32[1,8,8]{2,1,0:T(8,128)S(1)}, s32[1,8,8]{2,1,0:T(8,128)}, u32[]{:S(2)}) copy-start(s32[1,8,8]{2,1,0:T(8,128)} %su.1) | copy-start | bytes 772
  7.2 0.7 %copy-start.7 = (s32[1,8,8]{2,1,0:T(8,128)S(1)}, s32[1,8,8]{2,1,0:T(8,128)}, u32[]{:S(2)}) copy-start(s32[1,8,8]{2,1,0:T(8,128)} %sd.1) | copy-start | bytes 772
  7.9 0.7 %copy-start.8 = (s32[256]{0:T(256)S(1)}, s32[256]{0:T(256)}, u32[]{:S(2)}) copy-start(s32[256]{0:T(256)} %param.13) | copy-start | bytes 3076
  8.6 0.7 %copy-start.9 = (s32[1,4]{1,0:T(1,128)S(1)}, s32[1,4]{1,0:T(1,128)}, u32[]{:S(2)}) copy-start(s32[1,4]{1,0:T(1,128)} %counts.1) | copy-start | bytes 52
  9.3 0.7 %copy-start.10 = (s32[128,1]{0,1:T(1,128)S(1)}, s32[128,1]{0,1:T(1,128)}, u32[]{:S(2)}) copy-start(s32[128,1]{0,1:T(1,128)} %param.17) | copy-start | bytes 1540

commit v2 on v1

--- a/solution.py
+++ b/solution.py
@@ -97,8 +97,10 @@
 
 
 def fused(
-    cells, bins, counts, base, gain, ids, wg_hbm, wu_hbm, wd_hbm, sg, su, sd,
+    cells_hbm, bins_hbm, counts_hbm, base_hbm, gain_hbm, ids_hbm, wg_hbm, wu_hbm, wd_hbm,
+    sg_hbm, su_hbm, sd_hbm,
     out,
+    cells, bins, counts, base, gain, ids, sg, su, sd,
     wg, wu, wd, ids_mine, ids_sib, part, part_sib, part_x_out, part_x, resid, both,
     place, place_t, outgoing, rows_in, hidden, y32, y16, y_sib, q_out, q_in, final, back,
     send, recv, wsem,
@@ -116,7 +118,16 @@
         pltpu.make_async_copy(src.at[0], dst, wsem.at[n])
         for n, (src, dst) in enumerate(((wg_hbm, wg), (wu_hbm, wu), (wd_hbm, wd)))
     ]
-    for load in loads:
+    first = [
+        pltpu.make_async_copy(src, dst, wsem.at[3 + n])
+        for n, (src, dst) in enumerate(
+            (
+                (bins_hbm, bins), (counts_hbm, counts), (ids_hbm, ids), (cells_hbm, cells),
+                (base_hbm, base), (gain_hbm, gain), (sg_hbm, sg), (su_hbm, su), (sd_hbm, sd),
+            )
+        )
+    ]
+    for load in first + loads:
         load.start()
 
     barrier = pltpu.get_barrier_semaphore()
@@ -134,6 +145,8 @@
         )
 
     f32, bf16 = jnp.float32, jnp.bfloat16
+    for load in first[:4]:
+        load.wait()
     ids_mine[...] = jnp.broadcast_to(ids[...], (8, 128))
 
     cell_iota = lax.broadcasted_iota(jnp.int32, (1, 256), 1)
@@ -166,6 +179,8 @@
     part_x_out[...] = (cross + part_sib[0].astype(f32)).astype(bf16)
     c_px = rdma(part_x_out, part_x, 3, xpeer)
     c_px.start()
+    for load in first[4:]:
+        load.wait()
     resid[...] = base[...].astype(f32) + partial_of(2 * x + c)
 
     spread = (
@@ -360,6 +375,15 @@
     vmem, hbm = pl.BlockSpec(memory_space=pltpu.VMEM), pl.BlockSpec(memory_space=pl.ANY)
     d = 1024
     scratch = [
+        pltpu.VMEM(cells.shape, bf16),
+        pltpu.VMEM((1, 256), jnp.int32),
+        pltpu.VMEM((1, 4), jnp.int32),
+        pltpu.VMEM((128, d), bf16),
+        pltpu.VMEM((1, d), f32),
+        pltpu.VMEM((1, 128), jnp.int32),
+        pltpu.VMEM((1, 8, 8), jnp.int32),
+        pltpu.VMEM((1, 8, 8), jnp.int32),
+        pltpu.VMEM((1, 8, 8), jnp.int32),
         pltpu.VMEM((d, d), bf16),
         pltpu.VMEM((d, d), bf16),
         pltpu.VMEM((d, d), bf16),
@@ -385,16 +409,16 @@
         pltpu.VMEM((4, 2 * BLK, d), bf16),
         pltpu.SemaphoreType.DMA((NSEM,)),
         pltpu.SemaphoreType.DMA((NSEM,)),
-        pltpu.SemaphoreType.DMA((3,)),
+        pltpu.SemaphoreType.DMA((12,)),
     ]
     return pl.pallas_call(
         fused,
         out_shape=jax.ShapeDtypeStruct(bin_base.shape, bf16),
-        in_specs=[vmem] * 6 + [hbm] * 3 + [vmem] * 3,
+        in_specs=[hbm] * 12,
         out_specs=vmem,
         scratch_shapes=scratch,
         compiler_params=pltpu.CompilerParams(
-            collective_id=0, has_side_effects=True, vmem_limit_bytes=48 * 1024 * 1024
+            collective_id=0, has_side_effects=True, vmem_limit_bytes=64 * 1024 * 1024
         ),
         cost_estimate=pl.CostEstimate(
             flops=6 * 768 * d * d, bytes_accessed=8 * d * d, transcendentals=768 * d

time: 63.4 us -> 56.2 us (0.89)
  the two profiles are of different devices: /device:TPU:3 before, /device:TPU:0 now
where the time goes in v2:
time: 56.2 us; the launch traced here: 56.1 us
  Pallas kernels  54.4 us (97%)
  local copies, waits for them, and re-layouts  1.67 us (3%)
    pallas_call x1, Pallas kernels, on_device_fused(): pl.pallas_call(fused, out_shape=jax.ShapeDtypeStruct(bin_base.shape, bf16...  54.4 us
    unnamed x1, local copies, waits for them, and re-layouts  1.67 us

profile of v2, /device:TPU:0, one launch (start us, length us, event | category | flops | bytes accessed | tf_op | source)
XLA Modules:
  0.0 56.1 jit_solution(6432185296074279335)
XLA Ops:
  0.0 54.4 %shard_map.118 = bf16[128,1024]{1,0:T(8,128)(2,1)} custom-call(bf16[256,1024]{1,0:T(8,128)(2,1)} %cells_hbm.1, s32[1,256]{1,0:T(1,128)} %bitcast.4, s32[1,4]{1,0:T(1,128)} %counts_hbm.1, bf16[128,1024]{1,0:T(8,128)(2,1)} %base_hbm.1, f32[1,1024]{1,0:T(1,128)} %bitcast.3, s32[1,128]{1,0:T(1,128)} %bitcast.5, bf16[1,1024,1024]{2,1,0:T(8,128)(2,1)} %wg_hbm.1, ...), custom_call_target="tpu_custom_call" | custom-call | flops 4831838208 | bytes 8388608 | tf_op jit(solution)/shard_map/pallas_call | solution.py:414
  54.4 1.7 %copy.14 = bf16[128,1024]{1,0:T(8,128)(2,1)} copy(bf16[128,1024]{1,0:T(8,128)(2,1)} %shard_map.118) | data formatting | bytes 524288
